TPU v7x, 1024 devices: a whole 4x4x32 slice. The times are simulated.
1024 devices in a mesh: row: 32 (over z_lo, x), col: 32 (over z_hi, y, core).
Axes of the slice: x: 4, y: 4, z: 32 (z_hi: 4, z_lo: 8; z = z_hi * 8 + z_lo), core: 2. Of those that a mesh axis runs over, the one named last changes fastest.
Arguments:
- a_blocks: float32 [1024, 131072], P('row', 'col'), may hold values from -0.75 to 0.75
- b_blocks: float32 [1024, 131072], P('row', 'col'), may hold values from -6 to 6
- c_blocks: float32 [2048, 131072], P('row', 'col'), may hold values from -6 to 6
- stack_a: int32 [96, 2048], P('row', 'col'), may hold values from 0 to 31
- stack_b: int32 [96, 2048], P('row', 'col'), may hold values from 0 to 31
- stack_c: int32 [96, 2048], P('row', 'col'), may hold values from 0 to 63
- stack_len: int32 [96, 32], P('row', 'col'), may hold values from 8 to 64, as said below
Outputs:
- c_out: float32 [2048, 131072], P('row', 'col')
Inputs may be any that keep to these rules, and one draw needn't show every extreme that they name: `stack_len`: each stack length lies between 8 and 64; panel (0, 0) has full stacks in every phase.
All inputs are finite; a program needn't handle non-finite values.
Results may differ from a plain program's by a relative error of at most 0.0003.
Values sent between devices are 32-bit elements; how exact they have to be, the bound alone decides.
A program may use at most 32 MiB of HBM per device.

v0:
```python
import jax
import jax.numpy as jnp
from jax import lax
from jax.sharding import PartitionSpec as P

BLK = 64
STEPS = 2


def from_behind(value, axis, steps):
    count = lax.axis_size(axis)
    pairs = [(source, (source + steps) % count) for source in range(count)]
    return lax.ppermute(value, axis, pairs)


def phase_product(a_panel, b_panel, picks_a, picks_b, length, width):
    a_view = a_panel.reshape(a_panel.shape[0], width, width)
    b_view = b_panel.reshape(b_panel.shape[0], width, width)
    slots = jnp.arange(picks_a.shape[0], dtype=jnp.int32)
    live = (slots < length).astype(jnp.float32)
    picked_a = a_view[picks_a] * live[:, None, None]
    picked_b = b_view[picks_b]
    return jnp.einsum("kab,kbc->kac", picked_a, picked_b, precision=lax.Precision.HIGHEST)


def on_device(a_blocks, b_blocks, c_blocks, stack_a, stack_b, stack_c, stack_len):
    width = BLK
    slot_count = c_blocks.shape[0]
    total = c_blocks.reshape(slot_count, width, width)
    a_panel = a_blocks
    b_panel = b_blocks
    for phase in range(STEPS + 1):
        if phase > 0:
            a_panel = from_behind(a_panel, "col", -1)
            b_panel = from_behind(b_panel, "row", -1)
        product = phase_product(
            a_panel, b_panel, stack_a[phase], stack_b[phase], stack_len[phase, 0], width
        )
        total = total.at[stack_c[phase]].add(product)
    return total.reshape(slot_count, width * width)


def solution(mesh):
    placed = (
        P("row", "col"),
        P("row", "col"),
        P("row", "col"),
        P("row", "col"),
        P("row", "col"),
        P("row", "col"),
        P("row", "col"),
    )
    return jax.shard_map(
        on_device, mesh=mesh, in_specs=placed, out_specs=P("row", "col"), check_vma=False
    )
```

profile of v0, /device:TPU:6, one launch (start us, length us, event | category | flops | bytes accessed | tf_op | source)
XLA Modules:
  0.0 151.4 jit_solution(8448987750584243819)
XLA Ops:
  0.0 24.9 %collective-permute-start = (f32[32,4096]{1,0:T(8,128)}, f32[32,4096]{1,0:T(8,128)}, u32[]{:S(2)}, u32[]{:S(2)}) collective-permute-start(f32[32,4096]{1,0:T(8,128)} %param.7), channel_id=1, source_target_pairs={{0,31},{1,0},{2,1},{3,2},{4,3},{5,4},{6,5},{7,6},{8,7},{9,8},{10,9... | collective-permute-start | bytes 1572872 | tf_op jit(solution)/shard_map/ppermute | solution.py:13
  24.9 2.7 %collective-permute-start.1 = (f32[32,4096]{1,0:T(8,128)}, f32[32,4096]{1,0:T(8,128)}, u32[]{:S(2)}, u32[]{:S(2)}) collective-permute-start(f32[32,4096]{1,0:T(8,128)} %param.8), channel_id=1, source_target_pairs={{0,992},{32,0},{64,32},{96,64},{128,96},{160,128},{192,160},{224,1... | collective-permute-start | bytes 1572872 | tf_op jit(solution)/shard_map/ppermute | solution.py:13
  27.6 0.8 fusion.16
  28.4 0.8 fusion.17
  29.3 1.4 fusion.18
  31.2 0.8 fusion.15
  32.0 0.6 compare_convert_fusion.1
  32.7 1.5 reshape.292
  34.1 1.5 reshape.293
  35.6 2.0 %gather_fusion = f32[64,64,64]{2,1,0:T(8,128)} fusion(f32[32,64,64]{2,1,0:T(8,128)S(1)} %reshape.292, s32[1024]{0:T(1024)S(1)} %pad_clamp_fusion.5), kind=kCustom, calls=%fused_computation | custom fusion | bytes 2097408 | tf_op jit(solution)/shard_map/gather | solution.py:21
  37.6 2.0 %gather_fusion.1 = f32[64,64,64]{2,1,0:T(8,128)} fusion(f32[32,64,64]{2,1,0:T(8,128)S(1)} %reshape.293, s32[1024]{0:T(1024)S(1)} %pad_clamp_fusion.4), kind=kCustom, calls=%fused_computation.1 | custom fusion | bytes 2097408 | tf_op jit(solution)/shard_map/gather | solution.py:22
  39.6 5.2 %fusion.4 = f32[64,64,64]{2,1,0:T(8,128)} fusion(f32[64,64,64]{2,1,0:T(8,128)} %gather_fusion.1, f32[64,64,64]{2,1,0:T(8,128)S(1)} %copy-done, f32[64]{0:T(128)S(1)} %compare_convert_fusion.2), kind=kOutput, calls=%fused_computation.13 | convolution fusion | flops 201588736 | bytes 3145984 | tf_op jit(solution)/shard_map/kab,kbc->kac/dot_general | solution.py:23
  44.8 26.7 %collective-permute-done = f32[32,4096]{1,0:T(8,128)} collective-permute-done((f32[32,4096]{1,0:T(8,128)}, f32[32,4096]{1,0:T(8,128)}, u32[]{:S(2)}, u32[]{:S(2)}) %collective-permute-start) | collective-permute-done | bytes 524320 | tf_op jit(solution)/shard_map/ppermute | solution.py:13
  71.5 14.6 %collective-permute-start.2 = (f32[32,4096]{1,0:T(8,128)}, f32[32,4096]{1,0:T(8,128)}, u32[]{:S(2)}, u32[]{:S(2)}) collective-permute-start(f32[32,4096]{1,0:T(8,128)} %collective-permute-done), channel_id=1, source_target_pairs={{0,31},{1,0},{2,1},{3,2},{4,3},{5,4},{6,5},{7,6},{8,7},{9,8},{10,9... | collective-permute-start | bytes 1572872 | tf_op jit(solution)/shard_map/ppermute | solution.py:13
  86.2 2.9 %collective-permute-start.3 = (f32[32,4096]{1,0:T(8,128)}, f32[32,4096]{1,0:T(8,128)}, u32[]{:S(2)}, u32[]{:S(2)}) collective-permute-start(f32[32,4096]{1,0:T(8,128)} %collective-permute-done.1), channel_id=1, source_target_pairs={{0,992},{32,0},{64,32},{96,64},{128,96},{160,128},{192,160},{224,1... | collective-permute-start | bytes 1572872 | tf_op jit(solution)/shard_map/ppermute | solution.py:13
  89.1 0.7 compare_convert_fusion
  89.7 2.0 %reshape.291 = f32[64,64,64]{2,1,0:T(8,128)S(1)} reshape(f32[64,4096]{1,0:T(8,128)} %param.9) | data formatting | bytes 2097152 | tf_op jit(solution)/shard_map/reshape | solution.py:29
  91.8 7.0 %scatter_fusion = f32[64,64,64]{2,1,0:T(8,128)S(1)} fusion(f32[64,64,64]{2,1,0:T(8,128)S(1)} %reshape.291, s32[64]{0:T(128)S(1)} %get-tuple-element.12, f32[64,64,64]{2,1,0:T(8,128)} %fusion.4), kind=kCustom, calls=%fused_computation.6 | custom fusion | flops 262144 | bytes 3145984 | tf_op jit(solution)/shard_map/scatter-add | solution.py:39
  98.8 1.5 reshape.294
  100.2 2.0 %gather_fusion.2 = f32[64,64,64]{2,1,0:T(8,128)} fusion(f32[32,64,64]{2,1,0:T(8,128)S(1)} %reshape.294, s32[1024]{0:T(1024)S(1)} %pad_clamp_fusion.3), kind=kCustom, calls=%fused_computation.2 | custom fusion | bytes 2097408 | tf_op jit(solution)/shard_map/gather | solution.py:21
  102.2 1.5 reshape.295
  103.7 2.0 %gather_fusion.3 = f32[64,64,64]{2,1,0:T(8,128)} fusion(f32[32,64,64]{2,1,0:T(8,128)S(1)} %reshape.295, s32[1024]{0:T(1024)S(1)} %pad_clamp_fusion.2), kind=kCustom, calls=%fused_computation.3 | custom fusion | bytes 2097408 | tf_op jit(solution)/shard_map/gather | solution.py:22
  105.7 5.8 %fusion.2 = f32[64,64,64]{2,1,0:T(8,128)} fusion(f32[64,64,64]{2,1,0:T(8,128)} %gather_fusion.3, f32[64,64,64]{2,1,0:T(8,128)} %gather_fusion.2, f32[64]{0:T(128)S(1)} %compare_convert_fusion.1), kind=kOutput, calls=%fused_computation.11 | convolution fusion | flops 201588736 | bytes 3145984 | tf_op jit(solution)/shard_map/kab,kbc->kac/dot_general | solution.py:23
  111.6 7.0 %scatter_fusion.1 = f32[64,64,64]{2,1,0:T(8,128)S(1)} fusion(f32[64,64,64]{2,1,0:T(8,128)S(1)} %scatter_fusion, s32[64]{0:T(128)S(1)} %get-tuple-element.13, f32[64,64,64]{2,1,0:T(8,128)} %fusion.2), kind=kCustom, calls=%fused_computation.7 | custom fusion | flops 262144 | bytes 3145984 | tf_op jit(solution)/shard_map/scatter-add | solution.py:39
  118.6 1.5 reshape.296
  120.0 2.0 %gather_fusion.4 = f32[64,64,64]{2,1,0:T(8,128)} fusion(f32[32,64,64]{2,1,0:T(8,128)S(1)} %reshape.296, s32[1024]{0:T(1024)S(1)} %pad_clamp_fusion.1), kind=kCustom, calls=%fused_computation.4 | custom fusion | bytes 2097408 | tf_op jit(solution)/shard_map/gather | solution.py:21
  122.1 11.4 %collective-permute-done.3 = f32[32,4096]{1,0:T(8,128)} collective-permute-done((f32[32,4096]{1,0:T(8,128)}, f32[32,4096]{1,0:T(8,128)}, u32[]{:S(2)}, u32[]{:S(2)}) %collective-permute-start.3) | collective-permute-done | bytes 524320 | tf_op jit(solution)/shard_map/ppermute | solution.py:13
  133.5 1.5 reshape.297
  135.0 2.0 %gather_fusion.5 = f32[64,64,64]{2,1,0:T(8,128)} fusion(f32[32,64,64]{2,1,0:T(8,128)S(1)} %reshape.297, s32[1024]{0:T(1024)S(1)} %pad_clamp_fusion), kind=kCustom, calls=%fused_computation.5 | custom fusion | bytes 2097408 | tf_op jit(solution)/shard_map/gather | solution.py:22
  137.0 5.8 %fusion = f32[64,64,64]{2,1,0:T(8,128)} fusion(f32[64,64,64]{2,1,0:T(8,128)} %gather_fusion.5, f32[64,64,64]{2,1,0:T(8,128)} %gather_fusion.4, f32[64]{0:T(128)S(1)} %compare_convert_fusion), kind=kOutput, calls=%fused_computation.9 | convolution fusion | flops 201588736 | bytes 3145984 | tf_op jit(solution)/shard_map/kab,kbc->kac/dot_general | solution.py:23
  142.8 7.0 %scatter_fusion.2 = f32[64,64,64]{2,1,0:T(8,128)S(1)} fusion(f32[64,64,64]{2,1,0:T(8,128)S(1)} %scatter_fusion.1, s32[64]{0:T(128)S(1)} %get-tuple-element.11, f32[64,64,64]{2,1,0:T(8,128)} %fusion), kind=kCustom, calls=%fused_computation.8 | custom fusion | flops 262144 | bytes 3145984 | tf_op jit(solution)/shard_map/scatter-add | solution.py:39
  149.8 1.6 %reshape.298 = f32[64,4096]{1,0:T(8,128)} reshape(f32[64,64,64]{2,1,0:T(8,128)S(1)} %scatter_fusion.2) | data formatting | bytes 2097152 | tf_op jit(solution)/shard_map/reshape | solution.py:40
  (11 shorter events, 0.6 us)
Async XLA Ops:
  0.0 71.5 %collective-permute-start = (f32[32,4096]{1,0:T(8,128)}, f32[32,4096]{1,0:T(8,128)}, u32[]{:S(2)}, u32[]{:S(2)}) collective-permute-start(f32[32,4096]{1,0:T(8,128)} %param.7), channel_id=1, source_target_pairs={{0,31},{1,0},{2,1},{3,2},{4,3},{5,4},{6,5},{7,6},{8,7},{9,8},{10,9... | collective-permute-start | bytes 1572872 | tf_op jit(solution)/shard_map/ppermute | solution.py:13
  24.9 61.3 %collective-permute-start.1 = (f32[32,4096]{1,0:T(8,128)}, f32[32,4096]{1,0:T(8,128)}, u32[]{:S(2)}, u32[]{:S(2)}) collective-permute-start(f32[32,4096]{1,0:T(8,128)} %param.8), channel_id=1, source_target_pairs={{0,992},{32,0},{64,32},{96,64},{128,96},{160,128},{192,160},{224,1... | collective-permute-start | bytes 1572872 | tf_op jit(solution)/shard_map/ppermute | solution.py:13
  37.6 2.0 %copy-start = (f32[64,64,64]{2,1,0:T(8,128)S(1)}, f32[64,64,64]{2,1,0:T(8,128)}, u32[]{:S(2)}) copy-start(f32[64,64,64]{2,1,0:T(8,128)} %gather_fusion) | copy-start | bytes 3145732
  71.5 47.0 %collective-permute-start.2 = (f32[32,4096]{1,0:T(8,128)}, f32[32,4096]{1,0:T(8,128)}, u32[]{:S(2)}, u32[]{:S(2)}) collective-permute-start(f32[32,4096]{1,0:T(8,128)} %collective-permute-done), channel_id=1, source_target_pairs={{0,31},{1,0},{2,1},{3,2},{4,3},{5,4},{6,5},{7,6},{8,7},{9,8},{10,9... | collective-permute-start | bytes 1572872 | tf_op jit(solution)/shard_map/ppermute | solution.py:13
  86.2 47.4 %collective-permute-start.3 = (f32[32,4096]{1,0:T(8,128)}, f32[32,4096]{1,0:T(8,128)}, u32[]{:S(2)}, u32[]{:S(2)}) collective-permute-start(f32[32,4096]{1,0:T(8,128)} %collective-permute-done.1), channel_id=1, source_target_pairs={{0,992},{32,0},{64,32},{96,64},{128,96},{160,128},{192,160},{224,1... | collective-permute-start | bytes 1572872 | tf_op jit(solution)/shard_map/ppermute | solution.py:13
where the time goes:
time: 153 us; the launch traced here: 151 us
  starting transfers between devices  45.1 us (29%)
  waiting for transfers between devices  38.1 us (25%)
  local copies, waits for them, and re-layouts  25.8 us (17%)
  other arithmetic  25.3 us (17%)
  matrix products  16.9 us (11%)
    ppermute x4, starting transfers between devices, from_behind(): return lax.ppermute(value, axis, pairs)  45.1 us
    ppermute x4, waiting for transfers between devices, from_behind(): return lax.ppermute(value, axis, pairs)  38.1 us
    scatter-add x3, other arithmetic, on_device(): total = total.at[stack_c[phase]].add(product)  21 us
    dot_general x3, matrix products, phase_product(): jnp.einsum('kab,kbc->kac', picked_a, picked_b, precision=lax.Precision.HI...  16.9 us
    gather x3, local copies, waits for them, and re-layouts, phase_product(): picked_a = a_view[picks_a] * live[:, None, None]  6.06 us
    gather x3, local copies, waits for them, and re-layouts, phase_product(): picked_b = b_view[picks_b]  6.02 us
    reshape x3, local copies, waits for them, and re-layouts, phase_product(): b_view = b_panel.reshape(b_panel.shape[0], width, width)  4.36 us
    reshape x3, local copies, waits for them, and re-layouts, phase_product(): a_view = a_panel.reshape(a_panel.shape[0], width, width)  4.36 us
  transfers between devices with their start and end apart: 4, of which 2 were waited for; matrix products, arithmetic and copies ran while one was open for 33% of the time, Pallas kernels for 0%

commit v1 on v0

v1 whole, which is shorter than its diff:
```python
import functools

import jax
import jax.numpy as jnp
from jax import lax
from jax.experimental import pallas as pl
from jax.experimental.pallas import tpu as pltpu
from jax.sharding import PartitionSpec as P

MESH = pl.DeviceIdType.MESH
NX, NY, NZL, NZH = 4, 4, 8, 4
BLK = 64
LANES = 128
SUB = 8
PARTS = 4
F32, BF16 = jnp.float32, jnp.bfloat16


def on_left():
    return lax.broadcasted_iota(jnp.int32, (32, LANES), 1) < BLK


def halves(block):
    high = block.astype(BF16).astype(F32)
    rest = block - high
    left = on_left()
    even = jnp.where(left, high, pltpu.roll(rest, BLK, 1))
    odd = jnp.where(left, pltpu.roll(high, BLK, 1), rest)
    return even, odd


def split_a(panel, out, part):
    for s in range(SUB):
        even, odd = halves(panel[pl.ds(part * 256 + s, 32, stride=SUB), :])
        out[part * SUB + s, 0:32, :] = even.astype(BF16)
        out[part * SUB + s, 32:64, :] = odd.astype(BF16)


def split_b(panel, out, mixed, part):
    for s in range(SUB):
        even, odd = halves(panel[pl.ds(part * 256 + s, 32, stride=SUB), :])
        mixed[s, pl.ds(0, 32, stride=2), :] = even
        mixed[s, pl.ds(1, 32, stride=2), :] = odd
        out[part * SUB + s] = mixed[s].astype(BF16)


def multiply(phase, groups, sa_ref, sb_ref, fa, fb, prods):
    left = on_left()

    def body(g, carry):
        for s in range(SUB):
            e = g * SUB + s
            a = fa[sa_ref[phase, e]]
            b = fb[sb_ref[phase, e]]
            both = jnp.dot(a, jnp.concatenate([b, b], axis=0), preferred_element_type=F32)
            whole = both + pltpu.roll(both, BLK, 1)
            prods[pl.ds(g * 256 + s, 32, stride=SUB), :] = jnp.where(left, whole[0:32], whole[32:64])
        return carry

    lax.fori_loop(groups[0], groups[1], body, 0)


def spread(prods, spots, acc):
    def body(h, carry):
        for u in range(4):
            t = h * 4 + u
            rows = [prods[pl.ds(g * 256 + t * SUB, SUB), :] for g in range(8)]
            x = jnp.concatenate(rows, axis=0)
            high = x.astype(BF16)
            rest = (x - high.astype(F32)).astype(BF16)
            add = jnp.dot(spots, jnp.concatenate([high, rest], axis=0), preferred_element_type=F32)
            at = pl.ds(pl.multiple_of(t * LANES, LANES), LANES)
            acc[:, at] = acc[:, at] + add
        return carry

    lax.fori_loop(0, 8, body, 0)


def kernel(sa_ref, sb_ref, sl_ref, sc_ref, a_hbm, b_hbm, c_hbm, out_hbm,
           a_own, b_own, acc, a_next, a_side, b_one, b_two, relay, fa, fb, mixed, prods, spot,
           own_sem, a_send, a_recv, side_send, side_recv, b_send, b_recv, b2_send, b2_recv,
           rel_send, rel_recv, far_send, far_ok, wrap_ok):
    row, col = lax.axis_index("row"), lax.axis_index("col")
    x, zl = lax.rem(row, NX), lax.div(row, NX)
    core, y, zh = lax.rem(col, 2), lax.rem(lax.div(col, 2), NY), lax.div(col, 2 * NY)

    def at(y_, zh_):
        return (row, (lax.rem(zh_ + NZH, NZH) * NY + y_) * 2 + core)

    other = (row, col + 1 - 2 * core)
    up = (lax.rem(row + NX * NZL - 1, NX * NZL), col)
    down = (lax.rem(row + 1, NX * NZL), col)
    far = at(3, zh - 1)
    first_zh, last_zh = zh == 0, zh == NZH - 1
    wrap_from = row == 0
    wrap_to = row == NX * NZL - 1

    own = [
        pltpu.make_async_copy(a_hbm, a_own, own_sem.at[0]),
        pltpu.make_async_copy(b_hbm, b_own, own_sem.at[1]),
        pltpu.make_async_copy(c_hbm, acc, own_sem.at[2]),
    ]
    for copy in own:
        copy.start()

    barrier = pltpu.get_barrier_semaphore()

    def greet(device):
        pl.semaphore_signal(barrier, inc=1, device_id=device, device_id_type=MESH)

    @pl.when((y == 3) & jnp.logical_not(last_zh))
    def _():
        for k in range(NY):
            greet(at(k, zh + 1))

    @pl.when(first_zh)
    def _():
        greet(far)

    @pl.when(y >= 1)
    def _():
        greet(at(0, zh))

    @pl.when(y <= 2)
    def _():
        greet(at(y + 1, zh))

    greet(other)

    @pl.when(jnp.logical_not(wrap_to))
    def _():
        greet(down)

    @pl.when(wrap_from)
    def _():
        greet(up)

    expected = (1 + jnp.where(wrap_from, 0, 1) + jnp.where(wrap_to, 1, 0) + jnp.where(y == 0, 3, 1)
                + jnp.where(first_zh, 0, 1) + jnp.where((y == 3) & last_zh, NY, 0))
    pl.semaphore_wait(barrier, expected)

    @pl.when((y == 3) & last_zh)
    def _():
        for k in range(NY):
            pl.semaphore_signal(far_ok, inc=1, device_id=at(k, zh + 1), device_id_type=MESH)

    @pl.when(wrap_to)
    def _():
        pl.semaphore_signal(wrap_ok, inc=1, device_id=down, device_id_type=MESH)

    def quarter(ref, q):
        return ref.at[pl.ds(q * 256, 256)]

    def a_copy(q, device):
        return pltpu.make_async_remote_copy(quarter(a_hbm, q), quarter(a_next, q), a_send.at[q], a_recv.at[q],
                                            device_id=device, device_id_type=MESH)

    def relay_copy(q):
        return pltpu.make_async_remote_copy(quarter(a_hbm, q), relay, rel_send.at[q], rel_recv,
                                            device_id=at(q, zh), device_id_type=MESH)

    def far_copy(q):
        return pltpu.make_async_remote_copy(relay, quarter(a_next, q), far_send, a_recv.at[q],
                                            device_id=far, device_id_type=MESH)

    def side_copy(q, source):
        return pltpu.make_async_remote_copy(quarter(source, q), quarter(a_side, q), side_send.at[q], side_recv.at[q],
                                            device_id=other, device_id_type=MESH)

    def b_copy(q):
        return pltpu.make_async_remote_copy(quarter(b_hbm, q), quarter(b_one, q), b_send.at[q], b_recv.at[q],
                                            device_id=up, device_id_type=MESH)

    def b2_copy(q):
        return pltpu.make_async_remote_copy(quarter(b_one, q), quarter(b_two, q), b2_send.at[q], b2_recv.at[q],
                                            device_id=up, device_id_type=MESH)

    @pl.when(y == 0)
    def _():
        for q in (2, 1, 3):
            relay_copy(q).start()

        @pl.when(jnp.logical_not(first_zh))
        def _():
            a_copy(0, far).start()

    @pl.when(y >= 1)
    def _():
        for q in range(PARTS):
            a_copy(q, at(y - 1, zh)).start()

    @pl.when(jnp.logical_not(wrap_from))
    def _():
        for q in range(PARTS):
            b_copy(q).start()

    @pl.when(core == 1)
    def _():
        for q in range(PARTS):
            side_copy(q, a_hbm).start()

    def mark(phase):
        slot = lax.broadcasted_iota(jnp.int32, (BLK, BLK), 0)
        entry = lax.broadcasted_iota(jnp.int32, (BLK, BLK), 1)
        hit = (slot == sc_ref[phase:phase + 1, :]) & (entry < sl_ref[phase, 0])
        ones = jnp.where(hit, 1.0, 0.0)
        spot[:, 0:BLK] = ones
        spot[:, BLK:LANES] = ones

    def forward_relay():
        for q in range(1, PARTS):
            @pl.when(y == q)
            def _():
                relay_copy(q).wait_recv()
                far_copy(q).start()

    own[0].wait()
    for q in range(2):
        split_a(a_own, fa, q)

    @pl.when(jnp.logical_not(first_zh))
    def _():
        forward_relay()

    for q in range(2, PARTS):
        split_a(a_own, fa, q)
    own[1].wait()
    for q in range(PARTS):
        split_b(b_own, fb, mixed, q)
    mark(0)

    @pl.when(wrap_from)
    def _():
        pl.semaphore_wait(wrap_ok, 1)
        for q in range(PARTS):
            b_copy(q).start()

    for q in range(PARTS):
        multiply(0, (2 * q, 2 * q + 2), sa_ref, sb_ref, fa, fb, prods)
        b_copy(q).wait_recv()
        b2_copy(q).start()

    own[2].wait()
    spread(prods, spot[...].astype(BF16), acc)

    @pl.when(first_zh)
    def _():
        pl.semaphore_wait(far_ok, 1)

        @pl.when(y == 0)
        def _():
            a_copy(0, far).start()

        forward_relay()

    mark(1)
    for q in range(PARTS):
        split_b(b_one, fb, mixed, q)
    for q in range(PARTS):
        side_copy(q, a_hbm).wait_recv()
        split_a(a_side, fa, q)
    multiply(1, (0, 8), sa_ref, sb_ref, fa, fb, prods)
    spread(prods, spot[...].astype(BF16), acc)

    mark(2)
    for q in range(PARTS):
        b2_copy(q).wait_recv()
        split_b(b_two, fb, mixed, q)
    for q in range(PARTS):
        a_copy(q, far).wait_recv()

        @pl.when(core == 0)
        def _():
            side_copy(q, a_next).start()

    for q in range(PARTS):
        split_a(a_next, fa, q)
    multiply(2, (0, 8), sa_ref, sb_ref, fa, fb, prods)
    spread(prods, spot[...].astype(BF16), acc)
    result = pltpu.make_async_copy(acc, out_hbm, own_sem.at[0])
    result.start()

    for q in range(PARTS):
        side_copy(q, a_hbm).wait_send()
        b_copy(q).wait_send()
        b2_copy(q).wait_send()

    @pl.when(y == 0)
    def _():
        a_copy(0, far).wait_send()
        for q in (1, 2, 3):
            relay_copy(q).wait_send()

    @pl.when(y >= 1)
    def _():
        far_copy(0).wait_send()
        for q in range(PARTS):
            a_copy(q, far).wait_send()

    result.wait()


def tiles(panel):
    rows, cols = panel.shape
    view = panel.reshape(rows // SUB, SUB, cols // LANES, LANES).transpose(0, 2, 1, 3)
    return view.reshape(rows * cols // LANES, LANES)


def on_device(a_blocks, b_blocks, c_blocks, stack_a, stack_b, stack_c, stack_len):
    smem = pl.BlockSpec(memory_space=pltpu.SMEM)
    vmem = pl.BlockSpec(memory_space=pltpu.VMEM)
    hbm = pl.BlockSpec(memory_space=pl.ANY)
    panel = pltpu.VMEM((1024, LANES), F32)
    dma = pltpu.SemaphoreType.DMA
    return pl.pallas_call(
        kernel,
        out_shape=jax.ShapeDtypeStruct(c_blocks.shape, F32),
        in_specs=[smem, smem, smem, vmem, hbm, hbm, hbm],
        out_specs=hbm,
        scratch_shapes=[
            panel, panel, pltpu.VMEM((64, 4096), F32), panel, panel, panel, panel,
            pltpu.VMEM((256, LANES), F32),
            pltpu.VMEM((32, BLK, LANES), BF16), pltpu.VMEM((32, BLK, LANES), BF16),
            pltpu.VMEM((SUB, BLK, LANES), F32), pltpu.VMEM((2048, LANES), F32), pltpu.VMEM((BLK, LANES), F32),
            dma((3,)), dma((4,)), dma((4,)), dma((4,)), dma((4,)), dma((4,)), dma((4,)), dma((4,)), dma((4,)),
            dma((4,)), dma, dma, pltpu.SemaphoreType.REGULAR, pltpu.SemaphoreType.REGULAR,
        ],
        compiler_params=pltpu.CompilerParams(collective_id=0, has_side_effects=True, vmem_limit_bytes=32 * 2 ** 20),
        cost_estimate=pl.CostEstimate(flops=300_000_000, bytes_accessed=4_000_000, transcendentals=0),
    )(stack_a, stack_b, stack_len, stack_c, tiles(a_blocks), tiles(b_blocks), c_blocks)


def solution(mesh):
    placed = P("row", "col")
    return jax.shard_map(
        on_device, mesh=mesh, in_specs=(placed,) * 7, out_specs=placed, check_vma=False
    )
```

time: 153 us -> 73.5 us (0.48)
  the two profiles are of different devices: /device:TPU:6 before, /device:TPU:871 now
where the time goes in v1:
time: 73.5 us; the launch traced here: 73.2 us
  Pallas kernels  68.1 us (93%)
  local copies, waits for them, and re-layouts  5.06 us (7%)
    pallas_call x1, Pallas kernels, on_device(): pl.pallas_call(kernel, out_shape=jax.ShapeDtypeStruct(c_blocks.shape, F32...  68.1 us
    unnamed x14, local copies, waits for them, and re-layouts  5.06 us

profile of v1, /device:TPU:871, one launch (start us, length us, event | category | flops | bytes accessed | tf_op | source)
XLA Modules:
  0.0 73.2 jit_solution(7235999969811416941)
XLA Ops:
  0.0 0.0 copy-start.5
  0.0 0.0 copy-start.3
  0.0 0.0 copy-start.4
  0.0 0.8 %copy.8.sl_ref = s32[3,1]{1,0:T(4,128)S(1)} copy(s32[3,1]{0,1:T(1,128)} %param.13) | data formatting | bytes 24 | tf_op args[6]
  0.8 0.0 copy-done.5
  0.8 0.0 copy-done.3
  0.8 0.0 copy-done.4
  0.8 0.0 copy-start
  0.8 1.2 %copy-done = f32[64,4096]{1,0:T(8,128)S(1)} copy-done((f32[64,4096]{1,0:T(8,128)S(1)}, f32[64,4096]{1,0:T(8,128)}, u32[]{:S(2)}) %copy-start) | copy-done | bytes 1048600
  2.0 0.0 copy-start.1
  2.0 1.0 %copy-done.1 = f32[32,4096]{1,0:T(8,128)S(1)} copy-done((f32[32,4096]{1,0:T(8,128)S(1)}, f32[32,4096]{1,0:T(8,128)}, u32[]{:S(2)}) %copy-start.1) | copy-done | bytes 524312
  3.1 0.0 copy-start.2
  3.1 1.0 %copy-done.2 = f32[32,4096]{1,0:T(8,128)S(1)} copy-done((f32[32,4096]{1,0:T(8,128)S(1)}, f32[32,4096]{1,0:T(8,128)}, u32[]{:S(2)}) %copy-start.2) | copy-done | bytes 524312
  4.1 68.1 %shard_map.73 = f32[64,4096]{1,0:T(8,128)S(1)} custom-call(s32[3,64]{1,0:T(4,128)S(1)} %copy-done.3, s32[3,64]{1,0:T(4,128)S(1)} %copy-done.4, s32[3,1]{1,0:T(4,128)S(1)} %copy.8.sl_ref, s32[3,64]{1,0:T(4,128)S(1)} %copy-done.5, f32[1024,128]{1,0:T(8,128)S(1)} %bitcast.10, f32[1024,128]{1,0:T(8,128)S(1)} %bitcast.11, f32[64,4096]{1,0:T(8,128)S(1)} %copy-done), custom_call_target="tpu_custom_call" | custom-call | flops 300000000 | bytes 4000000 | tf_op jit(solution)/shard_map/pallas_call | solution.py:315
  72.2 1.0 %copy.10 = f32[64,4096]{1,0:T(8,128)} copy(f32[64,4096]{1,0:T(8,128)S(1)} %shard_map.73) | data formatting | bytes 2097152
Async XLA Ops:
  0.0 0.8 %copy-start.5 = (s32[3,64]{1,0:T(4,128)S(1)}, s32[3,64]{1,0:T(4,128)}, u32[]{:S(2)}) copy-start(s32[3,64]{1,0:T(4,128)} %sc_ref.1) | copy-start | bytes 2308
  0.0 0.8 %copy-start.3 = (s32[3,64]{1,0:T(4,128)S(1)}, s32[3,64]{1,0:T(4,128)}, u32[]{:S(2)}) copy-start(s32[3,64]{1,0:T(4,128)} %sa_ref.1) | copy-start | bytes 2308
  0.0 0.8 %copy-start.4 = (s32[3,64]{1,0:T(4,128)S(1)}, s32[3,64]{1,0:T(4,128)}, u32[]{:S(2)}) copy-start(s32[3,64]{1,0:T(4,128)} %sb_ref.1) | copy-start | bytes 2308
  0.8 1.2 %copy-start = (f32[64,4096]{1,0:T(8,128)S(1)}, f32[64,4096]{1,0:T(8,128)}, u32[]{:S(2)}) copy-start(f32[64,4096]{1,0:T(8,128)} %c_hbm.1) | copy-start | bytes 3145732
  2.0 1.0 %copy-start.1 = (f32[32,4096]{1,0:T(8,128)S(1)}, f32[32,4096]{1,0:T(8,128)}, u32[]{:S(2)}) copy-start(f32[32,4096]{1,0:T(8,128)} %param.7) | copy-start | bytes 1572868
  3.1 1.0 %copy-start.2 = (f32[32,4096]{1,0:T(8,128)S(1)}, f32[32,4096]{1,0:T(8,128)}, u32[]{:S(2)}) copy-start(f32[32,4096]{1,0:T(8,128)} %param.8) | copy-start | bytes 1572868

commit v2 on v1

v2 whole, which is shorter than its diff:
```python
import functools

import jax
import jax.numpy as jnp
from jax import lax
from jax.experimental import pallas as pl
from jax.experimental.pallas import tpu as pltpu
from jax.sharding import PartitionSpec as P

MESH = pl.DeviceIdType.MESH
NX, NY, NZL, NZH = 4, 4, 8, 4
BLK = 64
LANES = 128
SUB = 8
PARTS = 4
F32, BF16 = jnp.float32, jnp.bfloat16


def on_left():
    return lax.broadcasted_iota(jnp.int32, (32, LANES), 1) < BLK


def halves(block):
    high = block.astype(BF16).astype(F32)
    rest = block - high
    left = on_left()
    even = jnp.where(left, high, pltpu.roll(rest, BLK, 1))
    odd = jnp.where(left, pltpu.roll(high, BLK, 1), rest)
    return even, odd


def split_a(panel, out, part):
    for s in range(SUB):
        even, odd = halves(panel[pl.ds(part * 256 + s, 32, stride=SUB), :])
        out[part * SUB + s, 0:32, :] = even.astype(BF16)
        out[part * SUB + s, 32:64, :] = odd.astype(BF16)


def split_b(panel, out, mixed, part):
    for s in range(SUB):
        even, odd = halves(panel[pl.ds(part * 256 + s, 32, stride=SUB), :])
        mixed[s, pl.ds(0, 32, stride=2), :] = even
        mixed[s, pl.ds(1, 32, stride=2), :] = odd
        out[part * SUB + s] = mixed[s].astype(BF16)


def multiply(phase, first, groups, sa_ref, sb_ref, fa, fb, prods):
    left = on_left()

    def body(h, carry):
        for n in range(2 * SUB):
            g, s = h * 2 + n // SUB, n % SUB
            e = g * SUB + s
            a = fa[sa_ref[phase, e]]
            b = fb[sb_ref[phase, e]]
            both = jnp.dot(a, jnp.concatenate([b, b], axis=0), preferred_element_type=F32)
            whole = both + pltpu.roll(both, BLK, 1)
            prods[pl.ds(first + g * 256 + s, 32, stride=SUB), :] = jnp.where(left, whole[0:32], whole[32:64])
        return carry

    lax.fori_loop(groups[0] // 2, groups[1] // 2, body, 0)


def spread(prods, groups, spots, acc):
    def body(h, carry):
        for u in range(4):
            t = h * 4 + u
            rows = [prods[pl.ds(g * 256 + t * SUB, SUB), :] for g in range(groups)]
            x = jnp.concatenate(rows, axis=0)
            high = x.astype(BF16)
            rest = (x - high.astype(F32)).astype(BF16)
            add = jnp.dot(spots, jnp.concatenate([high, rest], axis=0), preferred_element_type=F32)
            at = pl.ds(pl.multiple_of(t * LANES, LANES), LANES)
            acc[:, at] = acc[:, at] + add
        return carry

    lax.fori_loop(0, 8, body, 0)


def kernel(sa_hbm, sb_hbm, sl_hbm, sc_hbm, a_hbm, b_hbm, c_hbm, acc,
           a_own, b_own, a_next, a_side, b_one, b_two, a_relay, b_relay, fa, fb, fa_two, fb_two, mixed, prods, spot,
           sa_ref, sb_ref, sl_ref, sc_ref,
           own_sem, a_send, a_recv, side_send, side_recv, b_send, b_recv, b2_send, b2_recv,
           rel_send, rel_recv, far_send, brel_send, brel_recv, bfar_send, far_ok, wrap_ok):
    row, col = lax.axis_index("row"), lax.axis_index("col")
    x, zl = lax.rem(row, NX), lax.div(row, NX)
    core, y, zh = lax.rem(col, 2), lax.rem(lax.div(col, 2), NY), lax.div(col, 2 * NY)

    def at(y_, zh_):
        return (row, (lax.rem(zh_ + NZH, NZH) * NY + y_) * 2 + core)

    def beside(x_, zl_):
        return (lax.rem(zl_ + NZL, NZL) * NX + x_, col)

    other = (row, col + 1 - 2 * core)
    far = at(3, zh - 1)
    above3, above2 = beside(3, zl - 1), beside(2, zl - 1)
    far_asks = (zh == 0) | (zh == NZH - 1)
    far_answers = (y == 3) & (zh >= NZH - 2)
    wrap_asks = zl == 0
    wrap_last = zl == NZL - 1

    sources = (sa_hbm, sb_hbm, sl_hbm, sc_hbm, a_hbm, b_hbm, c_hbm)
    places = (sa_ref, sb_ref, sl_ref, sc_ref, a_own, b_own, acc)
    own = [pltpu.make_async_copy(s_, d_, own_sem.at[n]) for n, (s_, d_) in enumerate(zip(sources, places))]

    barrier = pltpu.get_barrier_semaphore()

    def greet(device):
        pl.semaphore_signal(barrier, inc=1, device_id=device, device_id_type=MESH)

    @pl.when(far_asks)
    def _():
        greet(far)

    @pl.when(wrap_asks)
    def _():
        greet(above3)

        @pl.when(x != 1)
        def _():
            greet(above2)

    @pl.when((y == 3) & (zh < NZH - 2))
    def _():
        for k in range(NY):
            greet(at(k, zh + 1))

    @pl.when(y >= 1)
    def _():
        greet(at(0, zh))

    @pl.when(y <= 2)
    def _():
        greet(at(y + 1, zh))

    greet(other)

    for here, there in ((0, (1, 2)), (1, (2, 3)), (2, (3, 0, 1)), (3, (0,))):
        @pl.when(x == here)
        def _():
            for k in there:
                greet(beside(k, zl))

    for here, there in ((2, (0, 2, 3)), (3, (0, 1, 2, 3))):
        @pl.when((x == here) & jnp.logical_not(wrap_last))
        def _():
            for k in there:
                greet(beside(k, zl + 1))

    for copy in own[4:6] + own[:4] + own[6:]:
        copy.start()

    expected = (jnp.where(y == 0, 4, 2) + 2 + jnp.where(wrap_asks, 0, jnp.where(x == 1, 1, 2))
                + jnp.where(far_asks, 0, 1) + jnp.where(far_answers, NY, 0)
                + jnp.where(wrap_last, jnp.where(x == 3, 4, jnp.where(x == 2, 3, 0)), 0))
    pl.semaphore_wait(barrier, expected)

    @pl.when(far_answers)
    def _():
        for k in range(NY):
            pl.semaphore_signal(far_ok, inc=1, device_id=at(k, zh + 1), device_id_type=MESH)

    for here, there in ((2, (0, 2, 3)), (3, (0, 1, 2, 3))):
        @pl.when((x == here) & wrap_last)
        def _():
            for k in there:
                pl.semaphore_signal(wrap_ok, inc=1, device_id=beside(k, zl + 1), device_id_type=MESH)

    def quarter(ref, q):
        return ref.at[pl.ds(q * 256, 256)]

    def half(ref, q, h):
        return ref.at[pl.ds(q * 256 + h * 128, 128)]

    def send(source, target, send_sem, recv_sem, device):
        return pltpu.make_async_remote_copy(source, target, send_sem, recv_sem, device_id=device, device_id_type=MESH)

    def a_copy(q, h, device):
        return send(half(a_hbm, q, h), half(a_next, q, h), a_send.at[q, h], a_recv.at[q, h], device)

    def relay_copy(q, h):
        return send(half(a_hbm, q, h), half(a_relay, 0, h), rel_send.at[q, h], rel_recv.at[h], at(q, zh))

    def far_copy(q, h):
        return send(half(a_relay, 0, h), half(a_next, q, h), far_send.at[h], a_recv.at[q, h], far)

    def side_copy(q, source):
        return send(quarter(source, q), quarter(a_side, q), side_send.at[q], side_recv.at[q], other)

    def b_copy(q, device):
        return send(quarter(b_hbm, q), quarter(b_one, q), b_send.at[q], b_recv.at[q], device)

    def b2_copy(q, device):
        return send(quarter(b_hbm, q), quarter(b_two, q), b2_send.at[q], b2_recv.at[q], device)

    def b_relay_copy(q, slot, sem, device):
        return send(quarter(b_hbm, q), quarter(b_relay, slot), brel_send.at[sem], brel_recv.at[slot], device)

    def b_far_copy(sem, slot, q, target, recv, device):
        return send(quarter(b_relay, slot), quarter(target, q), bfar_send.at[sem], recv.at[q], device)

    @pl.when(y == 0)
    def _():
        for q in (2, 1, 3):
            for h in range(2):
                relay_copy(q, h).start()

    def send_above():
        @pl.when(x == 0)
        def _():
            b_copy(0, above3).start()
            b_copy(1, above3).start()
            b2_copy(0, above2).start()

        @pl.when(x == 1)
        def _():
            for q in range(3):
                b2_copy(q, above3).start()

    @pl.when(x == 0)
    def _():
        b_relay_copy(2, 1, 1, beside(3, zl)).start()
        b_relay_copy(3, 0, 2, beside(2, zl)).start()
        b_relay_copy(1, 0, 0, beside(3, zl)).start()

    @pl.when(x == 1)
    def _():
        b_relay_copy(3, 1, 0, beside(2, zl)).start()

    @pl.when(y >= 1)
    def _():
        for q in range(PARTS):
            for h in range(2):
                a_copy(q, h, at(y - 1, zh)).start()

    @pl.when(x >= 1)
    def _():
        for q in range(PARTS):
            b_copy(q, beside(x - 1, zl)).start()

    @pl.when(x >= 2)
    def _():
        for q in range(PARTS):
            b2_copy(q, beside(x - 2, zl)).start()

    @pl.when(core == 1)
    def _():
        for q in range(PARTS):
            side_copy(q, a_hbm).start()

    def forward_above():
        @pl.when(x == 2)
        def _():
            b_relay_copy(3, 0, 0, above3).wait_recv()
            b_far_copy(0, 0, 3, b_one, b_recv, above3).start()
            b_far_copy(1, 0, 3, b_two, b2_recv, above2).start()
            b_relay_copy(3, 1, 0, above3).wait_recv()
            b_far_copy(2, 1, 3, b_two, b2_recv, above3).start()

        @pl.when(x == 3)
        def _():
            b_relay_copy(2, 1, 0, above3).wait_recv()
            b_far_copy(1, 1, 2, b_one, b_recv, above3).start()
            b_far_copy(2, 1, 2, b_two, b2_recv, above2).start()
            b_relay_copy(1, 0, 0, above3).wait_recv()
            b_far_copy(0, 0, 1, b_two, b2_recv, above2).start()

    def far_start():
        @pl.when(far_asks)
        def _():
            pl.semaphore_wait(far_ok, 1)

        @pl.when(y == 0)
        def _():
            for h in range(2):
                a_copy(0, h, far).start()

        for q in range(1, PARTS):
            @pl.when(y == q)
            def _():
                for h in range(2):
                    relay_copy(q, h).wait_recv()
                    far_copy(q, h).start()

    def far_left():
        @pl.when(y == 0)
        def _():
            for h in range(2):
                a_copy(0, h, far).wait_send()

        @pl.when(y >= 1)
        def _():
            for h in range(2):
                far_copy(1, h).wait_send()

    def mark(phase, at_):
        slot = lax.broadcasted_iota(jnp.int32, (BLK, BLK), 0)
        entry = lax.broadcasted_iota(jnp.int32, (BLK, BLK), 1)
        hit = (slot == sc_ref[phase:phase + 1, :]) & (entry < sl_ref[0, phase])
        ones = jnp.where(hit, 1.0, 0.0)
        spot[:, at_:at_ + BLK] = ones

    @pl.when(jnp.logical_not(far_asks))
    def _():
        far_start()

    own[4].wait()
    for q in range(PARTS):
        split_a(a_own, fa, q)
    own[5].wait()
    for q in range(PARTS):
        split_b(b_own, fb, mixed, q)

    for copy in own[:4]:
        copy.wait()
    mark(0, 0)
    mark(0, BLK)
    multiply(0, 0, (0, 8), sa_ref, sb_ref, fa, fb, prods)
    own[6].wait()
    spread(prods, 8, spot[:, 0:LANES].astype(BF16), acc)

    @pl.when(wrap_asks)
    def _():
        pl.semaphore_wait(wrap_ok, jnp.where(x == 1, 1, 2))

    send_above()
    forward_above()

    @pl.when(far_asks)
    def _():
        far_start()


    for n in range(2):
        mark(1, n * LANES)
        mark(2, n * LANES + BLK)
    for q in range(PARTS):
        b_copy(q, other).wait_recv()
        split_b(b_one, fb, mixed, q)

    def phase_one():
        for q in range(PARTS):
            side_copy(q, a_hbm).wait_recv()
            split_a(a_side, fa, q)
        multiply(1, 0, (0, 8), sa_ref, sb_ref, fa, fb, prods)

    @pl.when(core == 0)
    def _():
        phase_one()

    for q in range(PARTS):
        b2_copy(q, other).wait_recv()
        split_b(b_two, fb_two, mixed, q)
    for q in range(PARTS):
        for h in range(2):
            a_copy(q, h, far).wait_recv()

        @pl.when(core == 0)
        def _():
            side_copy(q, a_next).start()

        split_a(a_next, fa_two, q)
    multiply(2, 2048, (0, 8), sa_ref, sb_ref, fa_two, fb_two, prods)

    @pl.when(core == 1)
    def _():
        phase_one()

    spread(prods, 16, spot[...].astype(BF16), acc)

    far_left()

    for q in range(PARTS):
        side_copy(q, a_hbm).wait_send()

    @pl.when(y == 0)
    def _():
        for q in (1, 2, 3):
            for h in range(2):
                relay_copy(q, h).wait_send()

    @pl.when(y >= 1)
    def _():
        for q in range(PARTS):
            for h in range(2):
                a_copy(q, h, far).wait_send()

    @pl.when(x == 0)
    def _():
        b_copy(0, other).wait_send()
        b_copy(1, other).wait_send()
        b2_copy(0, other).wait_send()
        for sem in range(3):
            b_relay_copy(0, 0, sem, other).wait_send()

    @pl.when(x >= 1)
    def _():
        for q in range(PARTS):
            b_copy(q, other).wait_send()
        for q in range(3):
            b2_copy(q, other).wait_send()

    @pl.when(x == 1)
    def _():
        b_relay_copy(0, 0, 0, other).wait_send()

    @pl.when(x >= 2)
    def _():
        b2_copy(3, other).wait_send()
        for sem in range(3):
            b_far_copy(sem, 0, 0, b_one, b_recv, other).wait_send()


def tiles(panel):
    rows, cols = panel.shape
    view = panel.reshape(rows // SUB, SUB, cols // LANES, LANES).transpose(0, 2, 1, 3)
    return view.reshape(rows * cols // LANES, LANES)


def on_device(a_blocks, b_blocks, c_blocks, stack_a, stack_b, stack_c, stack_len):
    hbm = pl.BlockSpec(memory_space=pl.ANY)
    panel = pltpu.VMEM((1024, LANES), F32)
    split = pltpu.VMEM((32, BLK, LANES), BF16)
    dma, flag = pltpu.SemaphoreType.DMA, pltpu.SemaphoreType.REGULAR
    picks = pltpu.SMEM(stack_a.shape, jnp.int32)
    return pl.pallas_call(
        kernel,
        out_shape=jax.ShapeDtypeStruct(c_blocks.shape, F32),
        in_specs=[hbm] * 7,
        out_specs=pl.BlockSpec(memory_space=pltpu.VMEM),
        scratch_shapes=[
            panel, panel, panel, panel, panel, panel, pltpu.VMEM((256, LANES), F32), pltpu.VMEM((512, LANES), F32),
            split, split, split, split,
            pltpu.VMEM((SUB, BLK, LANES), F32), pltpu.VMEM((4096, LANES), F32), pltpu.VMEM((BLK, 2 * LANES), F32),
            picks, picks, pltpu.SMEM(stack_len.shape[::-1], jnp.int32), pltpu.VMEM(stack_c.shape, jnp.int32),
            dma((7,)), dma((4, 2)), dma((4, 2)), dma((4,)), dma((4,)), dma((4,)), dma((4,)), dma((4,)), dma((4,)),
            dma((4, 2)), dma((2,)), dma((2,)), dma((3,)), dma((2,)), dma((3,)), flag, flag,
        ],
        compiler_params=pltpu.CompilerParams(collective_id=0, has_side_effects=True, vmem_limit_bytes=56 * 2 ** 20),
        cost_estimate=pl.CostEstimate(flops=300_000_000, bytes_accessed=4_000_000, transcendentals=0),
    )(stack_a, stack_b, stack_len.T, stack_c, tiles(a_blocks), tiles(b_blocks), c_blocks)


def solution(mesh):
    placed = P("row", "col")
    return jax.shard_map(
        on_device, mesh=mesh, in_specs=(placed,) * 7, out_specs=placed, check_vma=False
    )
```

time: 73.5 us -> 58.7 us (0.80)
  the two profiles are of different devices: /device:TPU:871 before, /device:TPU:575 now
where the time goes in v2:
time: 58.7 us; the launch traced here: 58.5 us
  Pallas kernels  56.2 us (96%)
  local copies, waits for them, and re-layouts  2.27 us (4%)
    pallas_call x1, Pallas kernels, on_device(): pl.pallas_call(kernel, out_shape=jax.ShapeDtypeStruct(c_blocks.shape, F32...  56.2 us
    unnamed x1, local copies, waits for them, and re-layouts  2.27 us

profile of v2, /device:TPU:575, one launch (start us, length us, event | category | flops | bytes accessed | tf_op | source)
XLA Modules:
  0.0 58.5 jit_solution(7009776541760440390)
XLA Ops:
  0.0 56.2 %shard_map.73 = f32[64,4096]{1,0:T(8,128)} custom-call(s32[3,64]{1,0:T(4,128)} %sa_hbm.1, s32[3,64]{1,0:T(4,128)} %sb_hbm.1, s32[1,3]{1,0:T(1,128)} %bitcast.13, s32[3,64]{1,0:T(4,128)} %sc_hbm.1, f32[1024,128]{1,0:T(8,128)} %bitcast.11, f32[1024,128]{1,0:T(8,128)} %bitcast.12, f32[64,4096]{1,0:T(8,128)} %c_hbm.1), custom_call_target="tpu_custom_call" | custom-call | flops 300000000 | bytes 4000000 | tf_op jit(solution)/shard_map/pallas_call | solution.py:427
  56.2 2.3 %copy.9 = f32[64,4096]{1,0:T(8,128)} copy(f32[64,4096]{1,0:T(8,128)} %shard_map.73) | data formatting | bytes 2097152

commit v3 on v2

--- a/solution.py
+++ b/solution.py
@@ -44,12 +44,12 @@
         out[part * SUB + s] = mixed[s].astype(BF16)
 
 
-def multiply(phase, first, groups, sa_ref, sb_ref, fa, fb, prods):
+def multiply(phase, first, wide, sa_ref, sb_ref, fa, fb, prods):
     left = on_left()
 
     def body(h, carry):
-        for n in range(2 * SUB):
-            g, s = h * 2 + n // SUB, n % SUB
+        for n in range(wide * SUB):
+            g, s = h * wide + n // SUB, n % SUB
             e = g * SUB + s
             a = fa[sa_ref[phase, e]]
             b = fb[sb_ref[phase, e]]
@@ -58,13 +58,13 @@
             prods[pl.ds(first + g * 256 + s, 32, stride=SUB), :] = jnp.where(left, whole[0:32], whole[32:64])
         return carry
 
-    lax.fori_loop(groups[0] // 2, groups[1] // 2, body, 0)
-
-
-def spread(prods, groups, spots, acc):
+    lax.fori_loop(0, 8 // wide, body, 0)
+
+
+def spread(prods, groups, wide, spots, acc):
     def body(h, carry):
-        for u in range(4):
-            t = h * 4 + u
+        for u in range(wide):
+            t = h * wide + u
             rows = [prods[pl.ds(g * 256 + t * SUB, SUB), :] for g in range(groups)]
             x = jnp.concatenate(rows, axis=0)
             high = x.astype(BF16)
@@ -74,7 +74,7 @@
             acc[:, at] = acc[:, at] + add
         return carry
 
-    lax.fori_loop(0, 8, body, 0)
+    lax.fori_loop(0, 32 // wide, body, 0)
 
 
 def kernel(sa_hbm, sb_hbm, sl_hbm, sc_hbm, a_hbm, b_hbm, c_hbm, acc,
@@ -316,9 +316,9 @@
         copy.wait()
     mark(0, 0)
     mark(0, BLK)
-    multiply(0, 0, (0, 8), sa_ref, sb_ref, fa, fb, prods)
+    multiply(0, 0, 1, sa_ref, sb_ref, fa, fb, prods)
     own[6].wait()
-    spread(prods, 8, spot[:, 0:LANES].astype(BF16), acc)
+    spread(prods, 8, 4, spot[:, 0:LANES].astype(BF16), acc)
 
     @pl.when(wrap_asks)
     def _():
@@ -343,7 +343,7 @@
         for q in range(PARTS):
             side_copy(q, a_hbm).wait_recv()
             split_a(a_side, fa, q)
-        multiply(1, 0, (0, 8), sa_ref, sb_ref, fa, fb, prods)
+        multiply(1, 0, 4, sa_ref, sb_ref, fa, fb, prods)
 
     @pl.when(core == 0)
     def _():
@@ -361,13 +361,13 @@
             side_copy(q, a_next).start()
 
         split_a(a_next, fa_two, q)
-    multiply(2, 2048, (0, 8), sa_ref, sb_ref, fa_two, fb_two, prods)
+    multiply(2, 2048, 4, sa_ref, sb_ref, fa_two, fb_two, prods)
 
     @pl.when(core == 1)
     def _():
         phase_one()
 
-    spread(prods, 16, spot[...].astype(BF16), acc)
+    spread(prods, 16, 16, spot[...].astype(BF16), acc)
 
     far_left()
 
@@ -426,7 +426,7 @@
     picks = pltpu.SMEM(stack_a.shape, jnp.int32)
     return pl.pallas_call(
         kernel,
-        out_shape=jax.ShapeDtypeStruct(c_blocks.shape, F32),
+        out_shape=pltpu.VMEM(c_blocks.shape, F32),
         in_specs=[hbm] * 7,
         out_specs=pl.BlockSpec(memory_space=pltpu.VMEM),
         scratch_shapes=[

time: 58.7 us -> 54.1 us (0.922)
  the two profiles are of different devices: /device:TPU:575 before, /device:TPU:767 now
where the time goes in v3:
time: 54.1 us; the launch traced here: 53.9 us
  Pallas kernels  52.9 us (98%)
  local copies, waits for them, and re-layouts  0.97 us (2%)
    pallas_call x1, Pallas kernels, on_device(): pl.pallas_call(kernel, out_shape=pltpu.VMEM(c_blocks.shape, F32), in_spec...  52.9 us

profile of v3, /device:TPU:767, one launch (start us, length us, event | category | flops | bytes accessed | tf_op | source)
XLA Modules:
  0.0 53.9 jit_solution(16676932790153444)
XLA Ops:
  0.0 52.9 %shard_map.73 = f32[64,4096]{1,0:T(8,128)S(1)} custom-call(s32[3,64]{1,0:T(4,128)} %sa_hbm.1, s32[3,64]{1,0:T(4,128)} %sb_hbm.1, s32[1,3]{1,0:T(1,128)} %bitcast.13, s32[3,64]{1,0:T(4,128)} %sc_hbm.1, f32[1024,128]{1,0:T(8,128)} %bitcast.11, f32[1024,128]{1,0:T(8,128)} %bitcast.12, f32[64,4096]{1,0:T(8,128)} %c_hbm.1), custom_call_target="tpu_custom_call" | custom-call | flops 300000000 | bytes 4000000 | tf_op jit(solution)/shard_map/pallas_call | solution.py:427
  52.9 1.0 %copy.9 = f32[64,4096]{1,0:T(8,128)} copy(f32[64,4096]{1,0:T(8,128)S(1)} %shard_map.73) | data formatting | bytes 2097152

commit v4 on v3

--- a/solution.py
+++ b/solution.py
@@ -228,44 +228,6 @@
     def _():
         b_relay_copy(3, 1, 0, beside(2, zl)).start()
 
-    @pl.when(y >= 1)
-    def _():
-        for q in range(PARTS):
-            for h in range(2):
-                a_copy(q, h, at(y - 1, zh)).start()
-
-    @pl.when(x >= 1)
-    def _():
-        for q in range(PARTS):
-            b_copy(q, beside(x - 1, zl)).start()
-
-    @pl.when(x >= 2)
-    def _():
-        for q in range(PARTS):
-            b2_copy(q, beside(x - 2, zl)).start()
-
-    @pl.when(core == 1)
-    def _():
-        for q in range(PARTS):
-            side_copy(q, a_hbm).start()
-
-    def forward_above():
-        @pl.when(x == 2)
-        def _():
-            b_relay_copy(3, 0, 0, above3).wait_recv()
-            b_far_copy(0, 0, 3, b_one, b_recv, above3).start()
-            b_far_copy(1, 0, 3, b_two, b2_recv, above2).start()
-            b_relay_copy(3, 1, 0, above3).wait_recv()
-            b_far_copy(2, 1, 3, b_two, b2_recv, above3).start()
-
-        @pl.when(x == 3)
-        def _():
-            b_relay_copy(2, 1, 0, above3).wait_recv()
-            b_far_copy(1, 1, 2, b_one, b_recv, above3).start()
-            b_far_copy(2, 1, 2, b_two, b2_recv, above2).start()
-            b_relay_copy(1, 0, 0, above3).wait_recv()
-            b_far_copy(0, 0, 1, b_two, b2_recv, above2).start()
-
     def far_start():
         @pl.when(far_asks)
         def _():
@@ -283,6 +245,43 @@
                     relay_copy(q, h).wait_recv()
                     far_copy(q, h).start()
 
+    @pl.when(jnp.logical_not(far_asks))
+    def _():
+        far_start()
+
+    @pl.when(y >= 1)
+    def _():
+        for q in range(PARTS):
+            for h in range(2):
+                a_copy(q, h, at(y - 1, zh)).start()
+
+    @pl.when(x >= 1)
+    def _():
+        for q in range(PARTS):
+            b_copy(q, beside(x - 1, zl)).start()
+
+    @pl.when(core == 1)
+    def _():
+        for q in range(PARTS):
+            side_copy(q, a_hbm).start()
+
+    def forward_above():
+        @pl.when(x == 2)
+        def _():
+            b_relay_copy(3, 0, 0, above3).wait_recv()
+            b_far_copy(0, 0, 3, b_one, b_recv, above3).start()
+            b_far_copy(1, 0, 3, b_two, b2_recv, above2).start()
+            b_relay_copy(3, 1, 0, above3).wait_recv()
+            b_far_copy(2, 1, 3, b_two, b2_recv, above3).start()
+
+        @pl.when(x == 3)
+        def _():
+            b_relay_copy(2, 1, 0, above3).wait_recv()
+            b_far_copy(1, 1, 2, b_one, b_recv, above3).start()
+            b_far_copy(2, 1, 2, b_two, b2_recv, above2).start()
+            b_relay_copy(1, 0, 0, above3).wait_recv()
+            b_far_copy(0, 0, 1, b_two, b2_recv, above2).start()
+
     def far_left():
         @pl.when(y == 0)
         def _():
@@ -300,10 +299,6 @@
         hit = (slot == sc_ref[phase:phase + 1, :]) & (entry < sl_ref[0, phase])
         ones = jnp.where(hit, 1.0, 0.0)
         spot[:, at_:at_ + BLK] = ones
-
-    @pl.when(jnp.logical_not(far_asks))
-    def _():
-        far_start()
 
     own[4].wait()
     for q in range(PARTS):
@@ -327,6 +322,11 @@
     send_above()
     forward_above()
 
+    @pl.when(x >= 2)
+    def _():
+        for q in range(PARTS):
+            b2_copy(q, beside(x - 2, zl)).start()
+
     @pl.when(far_asks)
     def _():
         far_start()
@@ -343,7 +343,7 @@
         for q in range(PARTS):
             side_copy(q, a_hbm).wait_recv()
             split_a(a_side, fa, q)
-        multiply(1, 0, 4, sa_ref, sb_ref, fa, fb, prods)
+        multiply(1, 0, 8, sa_ref, sb_ref, fa, fb, prods)
 
     @pl.when(core == 0)
     def _():
@@ -361,13 +361,13 @@
             side_copy(q, a_next).start()
 
         split_a(a_next, fa_two, q)
-    multiply(2, 2048, 4, sa_ref, sb_ref, fa_two, fb_two, prods)
+    multiply(2, 2048, 8, sa_ref, sb_ref, fa_two, fb_two, prods)
 
     @pl.when(core == 1)
     def _():
         phase_one()
 
-    spread(prods, 16, 16, spot[...].astype(BF16), acc)
+    spread(prods, 16, 32, spot[...].astype(BF16), acc)
 
     far_left()
 

time: 54.1 us -> 53.6 us (level)
  no operation moved by 1% of the time
where the time goes in v4:
time: 53.6 us; the launch traced here: 53.5 us
  Pallas kernels  52.5 us (98%)
  local copies, waits for them, and re-layouts  0.97 us (2%)
    pallas_call x1, Pallas kernels, on_device(): pl.pallas_call(kernel, out_shape=pltpu.VMEM(c_blocks.shape, F32), in_spec...  52.5 us

profile of v4, /device:TPU:767, one launch (start us, length us, event | category | flops | bytes accessed | tf_op | source)
XLA Modules:
  0.0 53.5 jit_solution(13251642966056288350)
XLA Ops:
  0.0 52.5 %shard_map.73 = f32[64,4096]{1,0:T(8,128)S(1)} custom-call(s32[3,64]{1,0:T(4,128)} %sa_hbm.1, s32[3,64]{1,0:T(4,128)} %sb_hbm.1, s32[1,3]{1,0:T(1,128)} %bitcast.13, s32[3,64]{1,0:T(4,128)} %sc_hbm.1, f32[1024,128]{1,0:T(8,128)} %bitcast.11, f32[1024,128]{1,0:T(8,128)} %bitcast.12, f32[64,4096]{1,0:T(8,128)} %c_hbm.1), custom_call_target="tpu_custom_call" | custom-call | flops 300000000 | bytes 4000000 | tf_op jit(solution)/shard_map/pallas_call | solution.py:427
  52.5 1.0 %copy.9 = f32[64,4096]{1,0:T(8,128)} copy(f32[64,4096]{1,0:T(8,128)S(1)} %shard_map.73) | data formatting | bytes 2097152
